TPU v7x, 32 devices: a whole 2x2x4 slice. The times are simulated.
32 devices in a mesh: seq: 8 (over z, x), head: 4 (over y, core).
Axes of the slice: x: 2, y: 2, z: 4, core: 2. Of those that a mesh axis runs over, the one named last changes fastest.
Arguments:
- tokens: bfloat16 [4096, 2048], P('seq'), may hold values from -6 to 6
- cotangent: bfloat16 [4096, 2048], P('seq'), may hold values from -6 to 6
- w_query: bfloat16 [2048, 2048], P(None, 'head'), may hold values from -0.61871843 to 0.61871843
- w_key: bfloat16 [2048, 2048], P(None, 'head'), may hold values from -0.61871843 to 0.61871843
- w_value: bfloat16 [2048, 2048], P(None, 'head'), may hold values from -0.61871843 to 0.61871843
- w_out: bfloat16 [2048, 2048], P('head'), may hold values from -0.61871843 to 0.61871843
- seeds: int32 [4], replicated, may hold values from 0 to 32748
Outputs:
- attended: bfloat16 [4096, 2048], P('seq', 'head')
- grad_tokens: bfloat16 [4096, 2048], P('seq', 'head')
- grad_w_query: float32 [2048, 2048], P('seq', 'head')
- grad_w_key: float32 [2048, 2048], P('seq', 'head')
- grad_w_value: float32 [2048, 2048], P('seq', 'head')
- grad_w_out: float32 [2048, 2048], P('head', 'seq')
All inputs are finite; a program needn't handle non-finite values.
Results may differ from a plain program's by a relative error of at most 0.013.
The roundings to bfloat16 on the way count: a program that leaves them out, or rounds other values in their place, can miss the bound.
Values may be sent and summed in bfloat16 or wider, within the bound.
A program may use at most 192 MiB of HBM per device.

v0:
```python
import functools
import math

import jax
import jax.numpy as jnp
import numpy as np
from jax import lax
from jax.experimental import pallas as pl
from jax.experimental.pallas import tpu as pltpu
from jax.sharding import PartitionSpec as P

DH = 128
LEAF = 128
LANES = 128

soft_cap = 6.0
noise_level = 0.5
prime_mod = 32749
inv_prime = 1.0 / prime_mod
BF = jnp.bfloat16
F32 = jnp.float32


def centre(residue):
    return jnp.where(residue > prime_mod // 2, residue - prime_mod, residue)


def dot32(left, right):
    return jnp.dot(left, right, preferred_element_type=F32)


def quotient(x, bias):
    return (x.astype(F32) * inv_prime - bias).astype(jnp.int32)


def perturb(axis_no, row_hash, row_base, col_hash, col_base, w_ref, out_ref):
    rows, cols = w_ref.shape
    chunk = min(rows, 256 if axis_no == 0 else 128)
    spread = None
    if axis_no == 0:

        def add_squares(i, total):
            part = w_ref[pl.ds(pl.multiple_of(i * chunk, chunk), chunk), :].astype(F32)
            return total + jnp.sum(part * part, axis=0, keepdims=True)

        squares = lax.fori_loop(0, rows // chunk, add_squares, jnp.zeros((1, cols), F32))
        spread = noise_level * jnp.sqrt(squares * (1.0 / rows) + 1e-06)

    def do_rows(i, carry):
        here = pl.ds(pl.multiple_of(i * chunk, chunk), chunk)
        r_hash = row_hash[here, :]
        r_id = lax.broadcasted_iota(jnp.int32, (chunk, LANES), 0) + (row_base + i * chunk)
        if axis_no == 0:
            base = spread
        else:
            whole = w_ref[here, :].astype(F32)
            mean = jnp.sum(whole * whole, axis=1, keepdims=True) * (1.0 / cols)
            base = noise_level * jnp.sqrt(mean + 1e-06)
        slope = base * (2.0 / (prime_mod - 1))
        for j in range(cols // LANES):
            at = slice(j * LANES, (j + 1) * LANES)
            c_id = lax.broadcasted_iota(jnp.int32, (1, LANES), 1) + (col_base + j * LANES)
            h = r_hash + col_hash[:, at]
            x = h * h + c_id
            h = x - quotient(x, 0.0) * prime_mod
            x = h * h + r_id
            h = x - quotient(x, 0.0078125) * prime_mod
            h = jnp.where(h >= prime_mod, h - prime_mod, h)
            step = slope[:, at] if axis_no == 0 else slope
            shift = base[:, at] if axis_no == 0 else base
            out_ref[here, at] = (w_ref[here, at].astype(F32) + (h.astype(F32) * step - shift)).astype(
                BF
            )
        return carry

    lax.fori_loop(0, rows // chunk, do_rows, 0)


def hash_rows(out_ref, row_base):
    rows = out_ref.shape[0]
    ids = lax.broadcasted_iota(jnp.int32, (rows, LANES), 0) + row_base
    x = ids * 7919
    out_ref[...] = centre(x - quotient(x, 0.0) * prime_mod)


def pair_mean(count):
    r = lax.broadcasted_iota(jnp.int32, (count // 2, count), 0)
    c = lax.broadcasted_iota(jnp.int32, (count // 2, count), 1)
    return jnp.where(c // 2 == r, 0.5, 0.0).astype(BF)


def coarse_levels(k_ref, v_ref, outs):
    cols = k_ref.shape[1]
    for n, src in enumerate((k_ref, v_ref)):
        rows = src[...]
        for out in outs:
            rows = dot32(pair_mean(rows.shape[0]), rows).astype(BF)
            out[:, n * cols : (n + 1) * cols] = rows


def attend(
    tok_rows,
    cross_rows,
    q_ref,
    k_ref,
    v_ref,
    do_ref,
    k1_ref,
    v1_ref,
    kx_ref,
    vx_ref,
    att_ref,
    dq_ref,
    dk_ref,
    dv_ref,
    dkvx_ref,
):
    pair = 2 * LEAF
    groups = tok_rows // pair
    scale_q = 1.0 / math.sqrt(DH)
    total_keys = pair + LEAF + cross_rows
    rows = lax.broadcasted_iota(jnp.int32, (total_keys, 1), 0)
    log_m = jnp.where(rows < pair, 0, (rows - pair) // LEAF + 1).astype(F32)
    dk1 = [None] * groups
    dv1 = [None] * groups
    dkx = None
    dvx = None
    for g in range(groups):
        own = slice(g * pair, (g + 1) * pair)
        other = slice((g ^ 1) * LEAF, ((g ^ 1) + 1) * LEAF)
        keys = jnp.concatenate([k_ref[own, :], k1_ref[other, :], kx_ref[...]], axis=0)
        values = jnp.concatenate([v_ref[own, :], v1_ref[other, :], vx_ref[...]], axis=0)
        q = q_ref[own, :]
        do = do_ref[own, :]
        do_t = do.astype(F32).T
        s = dot32(keys, q.astype(F32).T.astype(BF))
        t = jnp.tanh(s * (scale_q / soft_cap))
        w = jnp.exp2(t * (soft_cap * math.log2(math.e)) + log_m)
        weight_sum = jnp.sum(w, axis=0, keepdims=True)
        values_t = values.astype(F32).T.astype(BF)
        att_t = (dot32(values_t, w.astype(BF)) / weight_sum).astype(BF).astype(F32)
        att_ref[own, :] = att_t.T.astype(BF)
        delta = jnp.sum(att_t * do_t, axis=0, keepdims=True)
        p = w * (1.0 / weight_sum)
        dv = dot32(p.astype(BF), do)
        dp = dot32(values, do_t.astype(BF))
        grad = (p * (dp - delta) * (1.0 - t * t)).astype(BF)
        dk = dot32(grad, q) * scale_q
        keys_t = keys.astype(F32).T.astype(BF)
        dq_ref[own, :] = (dot32(keys_t, grad) * scale_q).T.astype(BF)
        dk_ref[own, :] = dk[:pair]
        dv_ref[own, :] = dv[:pair]
        dk1[g ^ 1] = dk[pair : pair + LEAF]
        dv1[g ^ 1] = dv[pair : pair + LEAF]
        dkx = dk[pair + LEAF :] if dkx is None else dkx + dk[pair + LEAF :]
        dvx = dv[pair + LEAF :] if dvx is None else dvx + dv[pair + LEAF :]
    r = lax.broadcasted_iota(jnp.int32, (pair, LEAF), 0)
    c = lax.broadcasted_iota(jnp.int32, (pair, LEAF), 1)
    expand = jnp.where(r // 2 == c, 0.5, 0.0).astype(BF)
    for g in range(groups):
        own = slice(g * pair, (g + 1) * pair)
        for ref, upper in ((dk_ref, dk1[g]), (dv_ref, dv1[g])):
            high = upper.astype(BF)
            low = (upper - high.astype(F32)).astype(BF)
            ref[own, :] += dot32(expand, high) + dot32(expand, low)
    dkvx_ref[0] = dkx.astype(BF)
    dkvx_ref[1] = dvx.astype(BF)


def cross_rows_of(apart):
    return LEAF >> (apart.bit_length() - 1)


def upper_matrix(tok_rows, seq_count):
    parts = []
    for apart in range(1, seq_count):
        count = cross_rows_of(apart)
        wide = tok_rows // count
        parts.append(np.kron(np.eye(count), np.ones((wide, 1))) / wide)
    return jnp.asarray(np.concatenate(parts, axis=1), BF)


def flipped(idx, apart):
    peer = idx
    for bit in range(apart.bit_length()):
        if apart >> bit & 1:
            peer = peer + (1 << bit) * (1 - 2 * (idx // (1 << bit) % 2))
    return peer


def dot_nt(left, right):
    return lax.dot_general(left, right, (((1,), (1,)), ((), ())), preferred_element_type=F32)


def remote(src, dst, send_sem, recv_sem, axis, peer):
    return pltpu.make_async_remote_copy(
        src_ref=src,
        dst_ref=dst,
        send_sem=send_sem,
        recv_sem=recv_sem,
        device_id={axis: peer},
        device_id_type=pl.DeviceIdType.MESH,
    )


def greet(axis, peer):
    pl.semaphore_signal(
        pltpu.get_barrier_semaphore(),
        inc=1,
        device_id={axis: peer},
        device_id_type=pl.DeviceIdType.MESH,
    )


def front_kernel(
    seq_count,
    tokens_hbm,
    cot_hbm,
    wq_hbm,
    wk_hbm,
    wv_hbm,
    wo_hbm,
    hq_ref,
    hk_ref,
    hv_ref,
    ho_ref,
    wq_ref,
    wk_ref,
    wv_ref,
    wo_ref,
    q_ref,
    k_ref,
    v_ref,
    do_ref,
    kv1_ref,
    kvx_ref,
    tok_pair_ref,
    tokens,
    cot,
    w_in,
    wo_in,
    all_hash,
    own_hash,
    tok_send,
    coarse,
    load,
    send,
    recv,
):
    seq_idx = lax.axis_index("seq")
    head_idx = lax.axis_index("head")
    tok_rows = tokens.shape[0]
    head_cols = k_ref.shape[1]
    outer, _, share = tok_send.shape
    inner = seq_idx % 2
    loads = [
        pltpu.make_async_copy(src, dst, load.at[n])
        for n, (src, dst) in enumerate(
            (
                (tokens_hbm, tokens),
                (wk_hbm, w_in.at[0]),
                (wv_hbm, w_in.at[1]),
                (wq_hbm, w_in.at[2]),
                (wo_hbm, wo_in),
                (cot_hbm, cot),
            )
        )
    ]
    for copy in loads:
        copy.start()
    barrier = pltpu.get_barrier_semaphore()
    for apart in range(1, seq_count):
        greet("seq", flipped(seq_idx, apart))
    hash_rows(all_hash, 0)
    hash_rows(own_hash, head_idx * head_cols)
    loads[0].wait()
    for c in range(outer):
        low = tokens[:, 2 * c * share : (2 * c + 1) * share]
        high = tokens[:, (2 * c + 1) * share : (2 * c + 2) * share]
        tok_send[c] = jnp.where(inner == 0, high, low)
    pl.semaphore_wait(barrier, seq_count - 1)
    tok_copy = remote(
        tok_send, tok_pair_ref, send.at[0], recv.at[0], "seq", flipped(seq_idx, 1)
    )
    tok_copy.start()

    block = min(tok_rows, 128)

    def project(src, w_ref, out_ref, form):
        def rows_at(i, carry):
            here = pl.ds(pl.multiple_of(i * block, block), block)
            out_ref[here, :] = form(src[here, :], w_ref[...]).astype(BF)
            return carry

        lax.fori_loop(0, tok_rows // block, rows_at, 0)

    own_base = head_idx * head_cols
    loads[1].wait()
    perturb(0, all_hash, 0, hk_ref, own_base, w_in.at[0], wk_ref)
    project(tokens, wk_ref, k_ref, dot32)
    loads[2].wait()
    perturb(0, all_hash, 0, hv_ref, own_base, w_in.at[1], wv_ref)
    project(tokens, wv_ref, v_ref, dot32)
    coarse_levels(k_ref, v_ref, [kv1_ref] + list(coarse))
    copies = []
    at = 0
    for apart in range(1, seq_count):
        count = cross_rows_of(apart)
        copies.append(
            remote(
                coarse[apart.bit_length() - 1],
                kvx_ref.at[pl.ds(at, count), :],
                send.at[apart],
                recv.at[apart],
                "seq",
                flipped(seq_idx, apart),
            )
        )
        at += count
    for copy in copies:
        copy.start()
    loads[3].wait()
    perturb(0, all_hash, 0, hq_ref, own_base, w_in.at[2], wq_ref)
    project(tokens, wq_ref, q_ref, dot32)
    loads[4].wait()
    perturb(1, own_hash, own_base, ho_ref, 0, wo_in, wo_ref)
    loads[5].wait()
    project(cot, wo_ref, do_ref, dot_nt)
    for copy in copies + [tok_copy]:
        copy.wait()


def front(seq_count, tokens, cotangent, weights, hashes):
    tok_rows, model_width = tokens.shape
    head_cols = weights[0].shape[1]
    outer, share = seq_count // 2, model_width // seq_count
    bits = seq_count.bit_length() - 1
    vmem = pl.BlockSpec(memory_space=pltpu.VMEM)
    hbm = pl.BlockSpec(memory_space=pl.ANY)
    dma = pltpu.SemaphoreType.DMA

    def array(*shape):
        return jax.ShapeDtypeStruct(shape, BF)

    cross_rows = sum(cross_rows_of(d) for d in range(1, seq_count))
    return pl.pallas_call(
        functools.partial(front_kernel, seq_count),
        in_specs=[hbm] * 6 + [vmem] * 4,
        out_specs=[vmem] * 11,
        out_shape=[array(*w.shape) for w in weights]
        + [array(tok_rows, head_cols)] * 4
        + [array(tok_rows // 2, 2 * head_cols), array(cross_rows, 2 * head_cols)]
        + [array(outer, tok_rows, share)],
        scratch_shapes=[
            pltpu.VMEM(tokens.shape, BF),
            pltpu.VMEM(tokens.shape, BF),
            pltpu.VMEM((3,) + weights[0].shape, BF),
            pltpu.VMEM(weights[3].shape, BF),
            pltpu.VMEM((model_width, LANES), jnp.int32),
            pltpu.VMEM((head_cols, LANES), jnp.int32),
            pltpu.VMEM((outer, tok_rows, share), BF),
            [pltpu.VMEM((tok_rows >> n + 2, 2 * head_cols), BF) for n in range(bits)],
            dma((6,)),
            dma((seq_count,)),
            dma((seq_count,)),
        ],
        compiler_params=pltpu.CompilerParams(
            collective_id=1, has_side_effects=True, vmem_limit_bytes=56 << 20
        ),
        cost_estimate=pl.CostEstimate(
            flops=8 * tok_rows * model_width * head_cols,
            bytes_accessed=32 << 20,
            transcendentals=0,
        ),
        name="front",
    )(tokens, cotangent, *weights, *hashes)


def tail_kernel(
    seq_count,
    head_count,
    q_ref,
    k_ref,
    v_ref,
    do_ref,
    kv1_ref,
    kvx_ref,
    upper_ref,
    tokens_ref,
    cot_ref,
    tok_pair_ref,
    wq_ref,
    wk_ref,
    wv_ref,
    wo_ref,
    attended_ref,
    grad_tok_ref,
    gq_ref,
    gk_ref,
    gv_ref,
    go_ref,
    att_ref,
    dq_ref,
    dk_own_ref,
    dv_own_ref,
    dkvx_ref,
    grads,
    pairs,
    tok_t,
    cot_t,
    tok_pair_t,
    half_out,
    half_in,
    back_in,
    head_out,
    head_in,
    chain_out,
    up_in,
    down_in,
    pair_send,
    pair_recv,
    dq_send,
    dq_recv,
    back_send,
    back_recv,
    head_send,
    head_recv,
    chain_send,
    up_recv,
    down_recv,
):
    seq_idx = lax.axis_index("seq")
    head_idx = lax.axis_index("head")
    outer = seq_count // 2
    z = seq_idx // 2
    inner = seq_idx % 2
    partner = flipped(seq_idx, 1)
    head_cols = att_ref.shape[1]

    outer_share = tok_pair_ref.shape[2]
    barrier = pltpu.get_barrier_semaphore()
    for apart in range(1, seq_count):
        greet("seq", flipped(seq_idx, apart))
    for apart in range(1, head_count):
        greet("head", (head_idx + apart) % head_count)
    pl.semaphore_wait(barrier, seq_count + head_count - 2)

    heads = head_cols // DH

    def head_columns(h, shift=0):
        return pl.ds(pl.multiple_of(h * DH + shift, DH), DH)

    def head_copies(h):
        cols = head_columns(h)
        copies = []
        at = 0
        for apart in range(1, seq_count):
            rows = pl.ds(at, cross_rows_of(apart))
            at += cross_rows_of(apart)
            copies.append(
                remote(
                    dkvx_ref.at[:, rows, cols],
                    back_in.at[:, rows, cols],
                    back_send.at[h, apart],
                    back_recv.at[h, apart],
                    "seq",
                    flipped(seq_idx, apart),
                )
            )
        copies.append(
            remote(
                dq_ref.at[:, cols],
                pairs.at[0, :, cols],
                dq_send.at[h],
                dq_recv.at[h],
                "seq",
                partner,
            )
        )
        return copies

    def one_head(h, carry):
        cols = head_columns(h)
        cross_cols = head_columns(h, head_cols)
        attend(
            q_ref.shape[0],
            kvx_ref.shape[0],
            q_ref.at[:, cols],
            k_ref.at[:, cols],
            v_ref.at[:, cols],
            do_ref.at[:, cols],
            kv1_ref.at[:, cols],
            kv1_ref.at[:, cross_cols],
            kvx_ref.at[:, cols],
            kvx_ref.at[:, cross_cols],
            att_ref.at[:, cols],
            dq_ref.at[:, cols],
            dk_own_ref.at[:, cols],
            dv_own_ref.at[:, cols],
            dkvx_ref.at[:, :, cols],
        )
        for copy in head_copies(h):
            copy.start()
        return carry

    sources = (dq_ref, att_ref, grads.at[0], grads.at[1])
    outs = (gq_ref, go_ref, gk_ref, gv_ref)
    pair_copies = [None] + [
        remote(
            half_out if n == 1 else sources[n],
            half_in if n == 1 else pairs.at[n],
            pair_send.at[n],
            pair_recv.at[n],
            "seq",
            partner,
        )
        for n in range(1, 4)
    ]

    def transpose_into(dst, src):
        width = min(256, src.shape[1])

        def columns(i, carry):
            here = pl.ds(pl.multiple_of(i * width, width), width)
            dst[here, :] = src[:, here].astype(F32).T.astype(BF)
            return carry

        lax.fori_loop(0, src.shape[1] // width, columns, 0)

    def own_rows(n, which):
        return pl.ds(pl.multiple_of((2 * n + which) * outer_share, outer_share), outer_share)

    def send_terms(which, term, result_ref):
        copies = []
        for apart in range(1, head_count):
            peer = (head_idx + apart) % head_count
            head_out[which, apart - 1] = term(peer).astype(BF)
            copy = remote(
                head_out.at[which, apart - 1],
                head_in.at[which, apart - 1],
                head_send.at[which, apart - 1],
                head_recv.at[which, apart - 1],
                "head",
                peer,
            )
            copy.start()
            copies.append(copy)
        return copies

    def finish_terms(which, term, copies, result_ref):
        total = term(head_idx)
        for apart, copy in enumerate(copies):
            copy.wait()
            total = total + head_in[which, apart].astype(F32)
        result_ref[...] = total.astype(BF)

    def piece(n):
        return pl.ds(pl.multiple_of(n * head_cols, head_cols), head_cols)

    def out_term(n):
        return dot32(att_ref[...], wo_ref[:, piece(n)])

    def in_term(n):
        return (
            dot_nt(dq_ref[...], wq_ref[piece(n), :])
            + dot_nt(grads[0], wk_ref[piece(n), :])
            + dot_nt(grads[1], wv_ref[piece(n), :])
        )

    def partial(n, c):
        if n == 1:
            return dot32(cot_t[own_rows(c, inner), :], att_ref[...]) + half_in[c].astype(F32)
        mine = dot32(tok_t[own_rows(c, inner), :], sources[n][...])
        return mine + dot32(tok_pair_t[c], pairs[n])

    def up_copy(n, c):
        return remote(
            chain_out.at[n, c], up_in.at[n, c], chain_send.at[n, c], up_recv.at[n, c],
            "seq", (seq_idx + 2) % seq_count,
        )

    def down_copy(n, c):
        return remote(
            chain_out.at[n, c], down_in.at[n, c], chain_send.at[n, c], down_recv.at[n, c],
            "seq", (seq_idx + seq_count - 2) % seq_count,
        )

    def chain(n):
        if n > 0:
            pair_copies[n].wait_recv()

        def step(t, carry):
            @pl.when(z <= t - 1)
            def _():
                c = z + outer - t
                chain_out[n, c] = partial(n, c).astype(BF)

                @pl.when(z > 0)
                def _():
                    up_copy(n, c).wait_recv()
                    chain_out[n, c] = (
                        chain_out[n, c].astype(F32) + up_in[n, c].astype(F32)
                    ).astype(BF)

                up_copy(n, c).start()

            @pl.when(z >= outer - t)
            def _():
                c = z + t - outer
                chain_out[n, c] = partial(n, c).astype(BF)

                @pl.when(z < outer - 1)
                def _():
                    down_copy(n, c).wait_recv()
                    chain_out[n, c] = (
                        chain_out[n, c].astype(F32) + down_in[n, c].astype(F32)
                    ).astype(BF)

                down_copy(n, c).start()

            return carry

        lax.fori_loop(1, outer, step, 0)

    def finish_chain(n):
        own = partial(n, z)

        def store(total):
            outs[n][...] = total.T if n == 1 else total

        @pl.when(z == 0)
        def _():
            down_copy(n, z).wait_recv()
            store(own + down_in[n, z].astype(F32))

        @pl.when(z == outer - 1)
        def _():
            up_copy(n, z).wait_recv()
            store(own + up_in[n, z].astype(F32))

        @pl.when((z > 0) & (z < outer - 1))
        def _():
            up_copy(n, z).wait_recv()
            down_copy(n, z).wait_recv()
            store(own + up_in[n, z].astype(F32) + down_in[n, z].astype(F32))

    lax.fori_loop(0, heads, one_head, 0)
    transpose_into(tok_t, tokens_ref)

    def transpose_pair(c, carry):
        tok_pair_t[c] = tok_pair_ref[c].astype(F32).T.astype(BF)
        return carry

    lax.fori_loop(0, outer, transpose_pair, 0)

    def head_arrived(h, carry):
        for copy in head_copies(h):
            copy.wait_recv()
        return carry

    lax.fori_loop(0, heads, head_arrived, 0)
    grads[0] = (dk_own_ref[...] + dot32(upper_ref[...], back_in[0])).astype(BF)
    pair_copies[2].start()
    grads[1] = (dv_own_ref[...] + dot32(upper_ref[...], back_in[1])).astype(BF)
    pair_copies[3].start()
    chain(0)
    att_copies = send_terms(0, out_term, attended_ref)
    transpose_into(cot_t, cot_ref)

    def send_half(c, carry):
        half_out[c] = dot32(cot_t[own_rows(c, 1 - inner), :], att_ref[...]).astype(BF)
        return carry

    lax.fori_loop(0, outer, send_half, 0)
    pair_copies[1].start()
    tok_copies = send_terms(1, in_term, grad_tok_ref)
    chain(2)
    finish_chain(0)
    chain(3)
    finish_terms(0, out_term, att_copies, attended_ref)
    finish_chain(2)
    chain(1)
    finish_terms(1, in_term, tok_copies, grad_tok_ref)
    finish_chain(3)
    finish_chain(1)
    for copy in pair_copies[1:]:
        copy.wait_send()

    def head_sent(h, carry):
        for copy in head_copies(h):
            copy.wait_send()
        return carry

    lax.fori_loop(0, heads, head_sent, 0)

    def drain(c, carry):
        @pl.when(c != z)
        def _():
            for n in range(4):
                up_copy(n, c).wait_send()

        return carry

    lax.fori_loop(0, outer, drain, 0)


def tail(seq_count, head_count, *arrays):
    queries, kvx, tokens, tok_pair = arrays[0], arrays[5], arrays[7], arrays[9]
    tok_rows, head_cols = queries.shape
    cross = (2, kvx.shape[0], head_cols)
    heads = head_cols // DH
    outer, _, share = tok_pair.shape
    vmem = pl.BlockSpec(memory_space=pltpu.VMEM)
    chunk = (4, outer, share, head_cols)
    grad = jax.ShapeDtypeStruct((share, head_cols), F32)
    tokens_out = jax.ShapeDtypeStruct((tok_rows, head_cols), BF)
    dma = pltpu.SemaphoreType.DMA
    return pl.pallas_call(
        functools.partial(tail_kernel, seq_count, head_count),
        in_specs=[vmem] * len(arrays),
        out_specs=[vmem] * 6,
        out_shape=[tokens_out] * 2
        + [grad] * 3
        + [jax.ShapeDtypeStruct((head_cols, share), F32)],
        scratch_shapes=[
            pltpu.VMEM((tok_rows, head_cols), BF),
            pltpu.VMEM((tok_rows, head_cols), BF),
            pltpu.VMEM((tok_rows, head_cols), F32),
            pltpu.VMEM((tok_rows, head_cols), F32),
            pltpu.VMEM(cross, BF),
            pltpu.VMEM((2, tok_rows, head_cols), BF),
            pltpu.VMEM((4, tok_rows, head_cols), BF),
            pltpu.VMEM(tokens.shape[::-1], BF),
            pltpu.VMEM(tokens.shape[::-1], BF),
            pltpu.VMEM((outer, share, tok_rows), BF),
            pltpu.VMEM((outer, share, head_cols), BF),
            pltpu.VMEM((outer, share, head_cols), BF),
            pltpu.VMEM(cross, BF),
            pltpu.VMEM((2, head_count - 1, tok_rows, head_cols), BF),
            pltpu.VMEM((2, head_count - 1, tok_rows, head_cols), BF),
            pltpu.VMEM(chunk, BF),
            pltpu.VMEM(chunk, BF),
            pltpu.VMEM(chunk, BF),
            dma((4,)),
            dma((4,)),
            dma((heads,)),
            dma((heads,)),
            dma((heads, seq_count)),
            dma((heads, seq_count)),
            dma((2, head_count - 1)),
            dma((2, head_count - 1)),
            dma((4, outer)),
            dma((4, outer)),
            dma((4, outer)),
        ],
        compiler_params=pltpu.CompilerParams(
            collective_id=0, has_side_effects=True, vmem_limit_bytes=60 << 20
        ),
        cost_estimate=pl.CostEstimate(
            flops=20 * tok_rows * head_cols * share * outer,
            bytes_accessed=32 << 20,
            transcendentals=0,
        ),
        name="tail",
    )(*arrays)


def settle_kernel(*refs):
    count = len(refs) // 2
    copies = [
        pltpu.make_async_copy(refs[n], refs[count + n], refs[-1].at[n]) for n in range(count)
    ]
    for copy in copies:
        copy.start()
    for copy in copies:
        copy.wait()


def settle(arrays):
    hbm = pl.BlockSpec(memory_space=pl.ANY)
    return pl.pallas_call(
        settle_kernel,
        in_specs=[hbm] * len(arrays),
        out_specs=[hbm] * len(arrays),
        out_shape=[jax.ShapeDtypeStruct(a.shape, a.dtype) for a in arrays],
        scratch_shapes=[pltpu.SemaphoreType.DMA((len(arrays),))],
        name="settle",
    )(*arrays)


def body(tokens, cotangent, w_query, w_key, w_value, w_out, seeds):
    seq_count = lax.axis_size("seq")
    head_count = lax.axis_size("head")
    head_idx = lax.axis_index("head")
    tok_rows, model_width = tokens.shape
    head_cols = w_query.shape[1]
    all_ids = jnp.arange(model_width, dtype=jnp.int32)
    own_ids = head_idx * head_cols + jnp.arange(head_cols, dtype=jnp.int32)

    def hash_cols(ids, seed):
        seeded = (ids * 10007 % prime_mod + seed * 31337 % prime_mod) % prime_mod
        return centre(seeded)[None, :]

    hashes = [hash_cols(own_ids, seeds[n]) for n in range(3)] + [hash_cols(all_ids, seeds[3])]
    (
        query_w,
        key_w,
        value_w,
        out_w,
        queries,
        keys,
        values,
        grad_att,
        kv1,
        kvx,
        tok_pair,
    ) = front(seq_count, tokens, cotangent, (w_query, w_key, w_value, w_out), hashes)
    return tuple(
        settle(
            tail(
                seq_count,
                head_count,
                queries,
                keys,
                values,
                grad_att,
                kv1,
                kvx,
                upper_matrix(tok_rows, seq_count),
                tokens,
                cotangent,
                tok_pair,
                query_w,
                key_w,
                value_w,
                out_w,
            )
        )
    )


def solution(mesh):
    in_specs = (
        P("seq", None),
        P("seq", None),
        P(None, "head"),
        P(None, "head"),
        P(None, "head"),
        P("head", None),
        P(),
    )
    out_specs = (
        P("seq", "head"),
        P("seq", "head"),
        P("seq", "head"),
        P("seq", "head"),
        P("seq", "head"),
        P("head", "seq"),
    )
    return jax.shard_map(body, mesh=mesh, in_specs=in_specs, out_specs=out_specs, check_vma=False)
```

profile of v0, /device:TPU:0, one launch (start us, length us, event | category | flops | bytes accessed | tf_op | source)
XLA Modules:
  0.0 258.9 jit_solution(15499840090830464792)
XLA Ops:
  0.6 1.4 fusion.2
  4.7 0.6 compare_select_fusion.3.hq_ref
  5.3 0.6 compare_select_fusion.1
  5.9 0.7 compare_select_fusion.ho_ref
  6.6 46.2 %front.1 = (bf16[2048,512]{1,0:T(8,128)(2,1)}, bf16[2048,512]{1,0:T(8,128)(2,1)}, bf16[2048,512]{1,0:T(8,128)(2,1)}, bf16[512,2048]{1,0:T(8,128)(2,1)}, bf16[512...) custom-call(bf16[512,2048]{1,0:T(8,128)(2,1)} %tokens_ref.1, ...), custom_call_target="tpu_custom_call" | custom-call | flops 4294967296 | bytes 33554432 | tf_op jit(solution)/shard_map/front/pallas_call | solution.py:346
  52.9 109.5 %tail.1 = (bf16[512,512]{1,0:T(8,128)(2,1)}, bf16[512,512]{1,0:T(8,128)(2,1)}, f32[256,512]{1,0:T(8,128)}, f32[256,512]{1,0:T(8,128)}, f32[256,512]{1,0:T(8,128)}, /*index=5*/f32[512,256]{1,0:T(8,128)}) custom-call(bf16[512,512]{1,0:T(8,128)(2,1)} %get-tuple-element.23.q_ref, bf16[512,512]{1,0:T(8,128)(2,1)} %get-tuple-element.24.k_ref, ...), custom_call_target="tpu_custom_call" | custom-call | flops 5368709120 | bytes 33554432 | tf_op jit(solution)/shard_map/tail/pallas_call | solution.py:718
  162.3 96.5 %settle.1 = (bf16[512,512]{1,0:T(8,128)(2,1)}, bf16[512,512]{1,0:T(8,128)(2,1)}, f32[256,512]{1,0:T(8,128)}, f32[256,512]{1,0:T(8,128)}, f32[256,512]{1,0:T(8,128)}, /*index=5*/f32[512,256]{1,0:T(8,128)}) custom-call(bf16[512,512]{1,0:T(8,128)(2,1)} %get-tuple-element.34.refs_0_, bf16[512,512]{1,0:T(8,128)(2,1)} %get-tuple-element.35.refs_1_, ...), custom_call_target="tpu_custom_call" | custom-call | tf_op jit(solution)/shard_map/settle/pallas_call | solution.py:781
where the time goes:
time: 259 us
  Pallas kernels  252 us (97%)
  between operations  3.47 us (1%)
    pallas_call x1, Pallas kernels, tail(): pl.pallas_call(functools.partial(tail_kernel, seq_count, head_count), in_...  109 us
    pallas_call x1, Pallas kernels, settle(): pl.pallas_call(settle_kernel, in_specs=[hbm] * len(arrays), out_specs=[hb...  96.5 us
    pallas_call x1, Pallas kernels, front(): pl.pallas_call(functools.partial(front_kernel, seq_count), in_specs=[hbm]...  46.2 us

commit v1 on v0

--- a/solution.py
+++ b/solution.py
@@ -499,8 +499,7 @@
             dv_own_ref.at[:, cols],
             dkvx_ref.at[:, :, cols],
         )
-        for copy in head_copies(h):
-            copy.start()
+        head_copies(h)[-1].start()
         return carry
 
     sources = (dq_ref, att_ref, grads.at[0], grads.at[1])
@@ -644,7 +643,13 @@
             down_copy(n, z).wait_recv()
             store(own + up_in[n, z].astype(F32) + down_in[n, z].astype(F32))
 
+    def send_back(h, carry):
+        for copy in head_copies(h)[:-1]:
+            copy.start()
+        return carry
+
     lax.fori_loop(0, heads, one_head, 0)
+    lax.fori_loop(0, heads, send_back, 0)
     transpose_into(tok_t, tokens_ref)
 
     def transpose_pair(c, carry):
@@ -653,17 +658,31 @@
 
     lax.fori_loop(0, outer, transpose_pair, 0)
 
-    def head_arrived(h, carry):
-        for copy in head_copies(h):
+    def dq_arrived(h, carry):
+        head_copies(h)[-1].wait_recv()
+        return carry
+
+    def back_arrived(h, carry):
+        for copy in head_copies(h)[:-1]:
             copy.wait_recv()
         return carry
 
-    lax.fori_loop(0, heads, head_arrived, 0)
+    lax.fori_loop(0, heads, dq_arrived, 0)
+
+    @pl.when((z == 0) | (z == outer - 1))
+    def _():
+        chain(0)
+
+    lax.fori_loop(0, heads, back_arrived, 0)
     grads[0] = (dk_own_ref[...] + dot32(upper_ref[...], back_in[0])).astype(BF)
     pair_copies[2].start()
     grads[1] = (dv_own_ref[...] + dot32(upper_ref[...], back_in[1])).astype(BF)
     pair_copies[3].start()
-    chain(0)
+
+    @pl.when((z > 0) & (z < outer - 1))
+    def _():
+        chain(0)
+
     att_copies = send_terms(0, out_term, attended_ref)
     transpose_into(cot_t, cot_ref)
 
@@ -767,23 +786,19 @@
 
 def settle_kernel(*refs):
     count = len(refs) // 2
-    copies = [
-        pltpu.make_async_copy(refs[n], refs[count + n], refs[-1].at[n]) for n in range(count)
-    ]
-    for copy in copies:
-        copy.start()
-    for copy in copies:
-        copy.wait()
+    for n in range(count):
+        refs[count + n][...] = refs[n][...]
 
 
 def settle(arrays):
-    hbm = pl.BlockSpec(memory_space=pl.ANY)
+    steps = 4
+    specs = [pl.BlockSpec((a.shape[0] // steps, a.shape[1]), lambda i: (i, 0)) for a in arrays]
     return pl.pallas_call(
         settle_kernel,
-        in_specs=[hbm] * len(arrays),
-        out_specs=[hbm] * len(arrays),
+        grid=(steps,),
+        in_specs=specs,
+        out_specs=specs,
         out_shape=[jax.ShapeDtypeStruct(a.shape, a.dtype) for a in arrays],
-        scratch_shapes=[pltpu.SemaphoreType.DMA((len(arrays),))],
         name="settle",
     )(*arrays)
 

time: 259 us -> 163 us (0.63)
  Pallas kernels: 252 us -> 156 us
    pallas_call x1, Pallas kernels: 96.5 us -> 4.23 us  [settle(): pl.pallas_call(settle_kernel, grid=(steps,), in_specs=specs, out_specs=sp...]
    pallas_call x1, Pallas kernels: 109 us -> 105 us  [tail(): pl.pallas_call(functools.partial(tail_kernel, seq_count, head_count), in_...]
where the time goes in v1:
time: 163 us; the launch traced here: 162 us
  Pallas kernels  156 us (96%)
  between operations  3.46 us (2%)
  other arithmetic  1.94 us (1%)
    pallas_call x1, Pallas kernels, tail(): pl.pallas_call(functools.partial(tail_kernel, seq_count, head_count), in_...  105 us
    pallas_call x1, Pallas kernels, front(): pl.pallas_call(functools.partial(front_kernel, seq_count), in_specs=[hbm]...  46.2 us
    pallas_call x1, Pallas kernels, settle(): pl.pallas_call(settle_kernel, grid=(steps,), in_specs=specs, out_specs=sp...  4.23 us

profile of v1, /device:TPU:0, one launch (start us, length us, event | category | flops | bytes accessed | tf_op | source)
XLA Modules:
  0.0 162.4 jit_solution(14987778876151846553)
XLA Ops:
  0.6 1.4 fusion.2
  4.7 0.6 compare_select_fusion.3.hq_ref
  5.3 0.6 compare_select_fusion.1
  5.9 0.7 compare_select_fusion.ho_ref
  6.6 46.2 %front.1 = (bf16[2048,512]{1,0:T(8,128)(2,1)}, bf16[2048,512]{1,0:T(8,128)(2,1)}, bf16[2048,512]{1,0:T(8,128)(2,1)}, bf16[512,2048]{1,0:T(8,128)(2,1)}, bf16[512...) custom-call(bf16[512,2048]{1,0:T(8,128)(2,1)} %tokens_ref.1, ...), custom_call_target="tpu_custom_call" | custom-call | flops 4294967296 | bytes 33554432 | tf_op jit(solution)/shard_map/front/pallas_call | solution.py:346
  52.9 105.2 %tail.1 = (bf16[512,512]{1,0:T(8,128)(2,1)}, bf16[512,512]{1,0:T(8,128)(2,1)}, f32[256,512]{1,0:T(8,128)}, f32[256,512]{1,0:T(8,128)}, f32[256,512]{1,0:T(8,128)}, /*index=5*/f32[512,256]{1,0:T(8,128)}) custom-call(bf16[512,512]{1,0:T(8,128)(2,1)} %get-tuple-element.23.q_ref, bf16[512,512]{1,0:T(8,128)(2,1)} %get-tuple-element.24.k_ref, ...), custom_call_target="tpu_custom_call" | custom-call | flops 5368709120 | bytes 33554432 | tf_op jit(solution)/shard_map/tail/pallas_call | solution.py:737
  158.1 4.2 %settle.1 = (bf16[512,512]{1,0:T(8,128)(2,1)}, bf16[512,512]{1,0:T(8,128)(2,1)}, f32[256,512]{1,0:T(8,128)}, f32[256,512]{1,0:T(8,128)}, f32[256,512]{1,0:T(8,128)}, /*index=5*/f32[512,256]{1,0:T(8,128)}) custom-call(bf16[512,512]{1,0:T(8,128)(2,1)} %get-tuple-element.34.refs_0_, bf16[512,512]{1,0:T(8,128)(2,1)} %get-tuple-element.35.refs_1_, ...), custom_call_target="tpu_custom_call" | custom-call | tf_op jit(solution)/shard_map/settle/pallas_call | solution.py:796
